TPU v7x, 32 devices: a whole 2x2x4 slice. The times are simulated.
32 devices in a mesh: segment: 4 (over x, core), field: 4 (over z), row: 2 (over y).
Axes of the slice: x: 2, y: 2, z: 4, core: 2. Of those that a mesh axis runs over, the one named last changes fastest.
Arguments:
- embeddings: bfloat16 [4, 256, 64, 256], P('segment', 'row', 'field'), may hold values from -6 to 6
- compress: bfloat16 [4, 64, 8], P('segment'), may hold values from -1.5 to 1.5
- mixing: bfloat16 [4, 512, 16384], P('segment', None, ('field', 'row')), may hold values from -0.25 to 0.25
- rescale_factor: float32 [4, 64, 256], P('segment', 'field'), may hold values from 0.5 to 1.5
- active_block_flags: int32 [4, 3], P('field'), may hold values from 1 to 3
Outputs:
- handed_on: bfloat16 [4, 256, 64, 256], P('segment', 'row', 'field')
All inputs are finite; a program needn't handle non-finite values.
Results may differ from a plain program's by a relative error of at most 0.013.
Values may be sent and summed in bfloat16 or wider, within the bound.
A program may use at most 128 MiB of HBM per device.

v0:
```python
import math

import jax
import jax.numpy as jnp
from jax import lax
from jax.sharding import PartitionSpec as P


def padded(array, sides, width):
    for axis, dim in sides:
        count, length = (lax.axis_size(axis), array.shape[dim])
        up = [(i, (i + 1) % count) for i in range(count)]
        down = [(j, i) for i, j in up]
        last = lax.slice_in_dim(array, length - width, length, axis=dim)
        initial = lax.slice_in_dim(array, 0, width, axis=dim)
        before = lax.ppermute(last, axis, up)
        after = lax.ppermute(initial, axis, down)
        array = jnp.concatenate([before, array, after], axis=dim)
    return array


def from_behind(array, axis, by):
    count = lax.axis_size(axis)
    return lax.ppermute(array, axis, [(i, (i + by) % count) for i in range(count)])


def squeeze_block(compress_rows, block_panel, block_index, field_dev):
    block_weights = lax.dynamic_slice_in_dim(compress_rows, block_index * field_dev, field_dev, 0)
    return jnp.einsum(
        "ak,rae->rke", block_weights, block_panel, preferred_element_type=jnp.float32
    ).astype(jnp.bfloat16)


def shards(embeddings, compress, mixing, rescale_factor, active_block_flags):
    own_panel = embeddings[0]
    device_rows, field_dev, feature_width = own_panel.shape
    owners = lax.axis_size("field")
    groups = lax.axis_size("row")
    myself = lax.axis_index("field")
    compress_rows = compress[0]
    rank_size = compress_rows.shape[1]
    beside_all = padded(own_panel[None], (("field", 0),), 1)
    reduced = jnp.stack(
        [
            squeeze_block(
                compress_rows,
                beside_all[offset_ordinal],
                (myself + offset_ordinal - 1 + owners) % owners,
                field_dev,
            )
            for offset_ordinal in range(3)
        ]
    )
    block_activity = active_block_flags[0].astype(jnp.float32)
    diagonal_block_products = jnp.einsum(
        "rae,drke->drak", own_panel, reduced, preferred_element_type=jnp.float32
    )
    pairwise_feature_product = (
        block_activity[0] * diagonal_block_products[0]
        + block_activity[1] * diagonal_block_products[1]
        + block_activity[2] * diagonal_block_products[2]
    )
    rank_rows = (
        (pairwise_feature_product * (1.0 / math.sqrt(feature_width)))
        .astype(jnp.bfloat16)
        .reshape(device_rows, field_dev * rank_size)
    )
    weights = mixing[0]
    block_span = field_dev * rank_size
    column_count = weights.shape[1]
    slabs = weights.reshape(owners, block_span, column_count)
    pieces = lax.all_gather(rank_rows[None], ("field", "row"), axis=0, tiled=True)
    member_count = pieces.shape[0]
    flat_index = jnp.arange(member_count, dtype=jnp.int32)
    owner_ids = flat_index // groups
    group_ids = flat_index % groups
    chosen = jnp.take(slabs, owner_ids, axis=0)
    contrib = jnp.einsum("mrc,mcd->mrd", pieces, chosen, preferred_element_type=jnp.float32)
    selector = (group_ids[:, None] == jnp.arange(groups, dtype=jnp.int32)[None, :]).astype(
        jnp.float32
    )
    placed = jnp.einsum("mg,mrd->grd", selector, contrib)
    projected = placed.reshape(groups * device_rows, column_count)
    fields_each = field_dev // groups
    local_mix = projected.astype(jnp.bfloat16).reshape(
        groups * device_rows, fields_each, feature_width
    )
    mixed_back = lax.all_to_all(local_mix, "row", split_axis=0, concat_axis=1, tiled=True)
    summed = own_panel.astype(jnp.float32) + mixed_back.astype(jnp.float32)
    mean_square = jnp.mean(summed * summed, axis=-1, keepdims=True)
    normed = (summed * lax.rsqrt(mean_square + 1e-06) * rescale_factor[0][None]).astype(
        jnp.bfloat16
    )
    handed = from_behind(normed, "segment", 1)
    return handed[None]


def solution(mesh):
    placed = (
        P("segment", "row", "field", None),
        P("segment", None, None),
        P("segment", None, ("field", "row")),
        P("segment", "field", None),
        P("field", None),
    )
    return jax.shard_map(
        shards,
        mesh=mesh,
        in_specs=placed,
        out_specs=P("segment", "row", "field", None),
        check_vma=False,
    )
```

profile of v0, /device:TPU:0, one launch (start us, length us, event | category | flops | bytes accessed | tf_op | source)
XLA Modules:
  0.0 126.9 jit_solution(6650759970934596916)
XLA Ops:
  0.0 0.0 copy-start
  0.0 3.0 %collective-permute-start = (bf16[1,128,16,256]{3,2,1,0:T(8,128)(2,1)}, bf16[1,128,16,256]{3,2,1,0:T(8,128)(2,1)}, u32[]{:S(2)}, u32[]{:S(2)}) collective-permute-start(bf16[1,128,16,256]{3,2,1,0:T(8,128)(2,1)} %param.5), channel_id=1, source_target_pairs={{0,2},{2,4},{4,6},{6,0},{1,3},{3,5},{5,7},{7,1},{8,10},{10,12},{12... | collective-permute-start | bytes 3145736 | tf_op jit(solution)/shard_map/ppermute | solution.py:16
  3.0 2.1 %collective-permute-start.1 = (bf16[1,128,16,256]{3,2,1,0:T(8,128)(2,1)}, bf16[1,128,16,256]{3,2,1,0:T(8,128)(2,1)}, u32[]{:S(2)}, u32[]{:S(2)}) collective-permute-start(bf16[1,128,16,256]{3,2,1,0:T(8,128)(2,1)} %param.5), channel_id=1, source_target_pairs={{2,0},{4,2},{6,4},{0,6},{3,1},{5,3},{7,5},{1,7},{10,8},{12,10},{14... | collective-permute-start | bytes 3145736 | tf_op jit(solution)/shard_map/ppermute | solution.py:17
  5.1 0.7 convert_element_type.57
  5.8 0.0 copy-done
  5.8 0.0 copy-start.1
  5.8 0.0 copy-start.3
  5.8 2.8 %gather_fusion = bf16[8,128,2048]{2,1,0:T(8,128)(2,1)} fusion(bf16[4,128,2048]{2,1,0:T(8,128)(2,1)S(1)} %bitcast.70, s32[1024]{0:T(1024)S(1)} %pad_clamp_fusion), kind=kCustom, calls=%fused_computation | custom fusion | bytes 8388640 | tf_op jit(solution)/shard_map/jit(_take)/gather | solution.py:77
  8.6 0.6 fusion.38
  9.2 0.0 copy-done.1
  9.2 0.0 copy-done.3
  9.2 0.4 fusion.12
  9.6 19.8 %collective-permute-done = bf16[1,128,16,256]{3,2,1,0:T(8,128)(2,1)} collective-permute-done((bf16[1,128,16,256]{3,2,1,0:T(8,128)(2,1)}, bf16[1,128,16,256]{3,2,1,0:T(8,128)(2,1)}, u32[]{:S(2)}, u32[]{:S(2)}) %collective-permute-start) | collective-permute-done | bytes 1048608 | tf_op jit(solution)/shard_map/ppermute | solution.py:16
  29.4 1.6 %fusion.11 = bf16[1,128,8,256]{3,2,1,0:T(8,128)(2,1)S(1)} fusion(bf16[1,128,16,256]{3,2,1,0:T(8,128)(2,1)} %collective-permute-done, bf16[1,64,8]{1,2,0:T(8,128)(2,1)S(1)} %copy-done.3, s32[]{:T(128)S(6)} %select_n.71), kind=kOutput, calls=%fused_computation.18 | convolution fusion | flops 8650752 | bytes 1573892 | tf_op jit(solution)/shard_map/ak,rae->rke/dot_general | solution.py:29
  31.0 19.5 %collective-permute-done.1 = bf16[1,128,16,256]{3,2,1,0:T(8,128)(2,1)} collective-permute-done((bf16[1,128,16,256]{3,2,1,0:T(8,128)(2,1)}, bf16[1,128,16,256]{3,2,1,0:T(8,128)(2,1)}, u32[]{:S(2)}, u32[]{:S(2)}) %collective-permute-start.1) | collective-permute-done | bytes 1048608 | tf_op jit(solution)/shard_map/ppermute | solution.py:17
  50.4 1.6 %fusion.13 = bf16[1,128,8,256]{3,2,1,0:T(8,128)(2,1)S(1)} fusion(bf16[1,128,16,256]{3,2,1,0:T(8,128)(2,1)} %collective-permute-done.1, bf16[1,64,8]{1,2,0:T(8,128)(2,1)S(1)} %copy-done.3, s32[]{:T(128)S(6)} %select_n.75), kind=kOutput, calls=%fused_computation.20 | convolution fusion | flops 8650752 | bytes 1573892 | tf_op jit(solution)/shard_map/ak,rae->rke/dot_general | solution.py:29
  52.0 1.7 %fusion.9 = f32[128,3,8,16]{3,2,1,0:T(8,128)} fusion(bf16[1,128,16,256]{3,2,1,0:T(8,128)(2,1)S(1)} %copy-done.1, bf16[1,128,8,256]{3,2,1,0:T(8,128)(2,1)S(1)} %fusion.13, bf16[1,128,8,256]{3,2,1,0:T(8,128)(2,1)S(1)} %fusion.12, bf16[1,128,8,256]{3,2,1,0:T(8,128)(2,1)S(1)} %fusion.11), kind=kOutput, calls=%fused_computation.13 | convolution fusion | flops 26738688 | bytes 2818048 | tf_op jit(solution)/shard_map/rae,drke->drak/dot_general | solution.py:55
  53.7 1.8 %copy.30 = f32[128,3,8,16]{0,2,3,1:T(8,128)S(1)} copy(f32[128,3,8,16]{3,2,1,0:T(8,128)} %fusion.9) | data formatting | bytes 393216 | tf_op jit(solution)/shard_map/rae,drke->drak/dot_general | solution.py:55
  55.6 1.9 %fusion.22 = bf16[1,128,128]{1,2,0:T(8,128)(2,1)S(1)} fusion(f32[3,128,16,8]{1,3,2,0:T(8,128)S(1)} %bitcast.76, f32[]{:T(128)} %bitcast.21, f32[]{:T(128)} %bitcast.20, f32[]{:T(128)} %bitcast.2), kind=kLoop, calls=%fused_computation.32 | loop fusion | flops 114688 | bytes 229388 | tf_op jit(solution)/shard_map/mul | solution.py:64
  57.5 0.1 copy.31
  57.6 31.4 %all_gather.3 = bf16[8,128,128]{2,1,0:T(8,128)(2,1)S(1)} all-gather(bf16[1,128,128]{2,1,0:T(8,128)(2,1)S(1)} %copy.31), channel_id=1, replica_groups=mesh['segment'=4,'field'=4,'row'=2] {'field','row'}, dimensions={0}, use_global_device_ids=true | all-gather | bytes 294912 | tf_op jit(solution)/shard_map/all_gather | solution.py:72
  89.0 3.5 %fusion.2 = bf16[8,128,2048]{2,1,0:T(8,128)(2,1)S(1)} fusion(bf16[8,128,128]{2,1,0:T(8,128)(2,1)S(1)} %all_gather.3, bf16[8,128,2048]{2,1,0:T(8,128)(2,1)} %gather_fusion, pred[8]{0:T(512)(128)(4,1)S(1)} %compare_and_fusion), kind=kOutput, calls=%fused_computation.3 | convolution fusion | flops 538968064 | bytes 8650760 | tf_op jit(solution)/shard_map/mrc,mcd->mrd/dot_general | solution.py:78
  92.5 3.1 %fusion.5 = bf16[2,128,2048]{2,0,1:T(2,128)(2,1)S(1)} fusion(bf16[8,128,2048]{2,1,0:T(8,128)(2,1)S(1)} %fusion.2, s32[8]{0:T(128)S(1)} %and_select_fusion.2), kind=kOutput, calls=%fused_computation.6 | convolution fusion | flops 8388624 | bytes 5242912 | tf_op jit(solution)/shard_map/mg,mrd->grd/dot_general | solution.py:82
  95.6 0.4 copy.33
  95.9 0.3 copy.38
  96.2 0.0 copy-start.4
  96.2 12.2 %all_to_all.4 = bf16[256,8,256]{2,1,0:T(8,128)(2,1)S(1)} all-to-all(bf16[256,8,256]{2,1,0:T(8,128)(2,1)S(1)} %bitcast.74), channel_id=1, replica_groups=mesh['segment'=4,'field'=4,'row'=2] {'row'}, dimensions={0} | all-to-all | bytes 2097152 | tf_op jit(solution)/shard_map/all_to_all | solution.py:88
  108.4 0.0 copy-start.2
  108.4 1.0 copy-done.2
  109.4 0.4 multiply_reduce_fusion
  109.8 0.1 copy.35
  109.9 0.1 copy.36
  110.0 0.0 copy-done.4
  110.0 1.6 %multiply_convert_fusion = bf16[128,16,256]{2,1,0:T(8,128)(2,1)S(1)} fusion(bf16[1,128,16,256]{3,2,1,0:T(8,128)(2,1)S(1)} %copy-done.1, f32[16,256]{1,0:T(8,128)S(1)} %bitcast.77, f32[128,16]{1,0:T(8,128)S(1)} %copy.36, bf16[2,128,8,256]{3,2,1,0:T(8,128)(2,1)} %bitcast.72), kind=kLoop, calls=%fused_computation.9 | loop fusion | flops 3145728 | bytes 3170304 | tf_op jit(solution)/shard_map/convert_element_type | solution.py:91
  111.6 0.1 collective-permute-start.2
  111.7 14.2 %collective-permute-done.2 = bf16[128,16,256]{2,1,0:T(8,128)(2,1)S(1)} collective-permute-done((bf16[128,16,256]{2,1,0:T(8,128)(2,1)S(1)}, bf16[128,16,256]{2,1,0:T(8,128)(2,1)S(1)}, u32[]{:S(2)}, u32[]{:S(2)}) %collective-permute-start.2) | collective-permute-done | bytes 1048608 | tf_op jit(solution)/shard_map/ppermute | solution.py:24
  125.9 1.0 copy.51
  (5 shorter events, 0.0 us)
Async XLA Ops:
  0.0 5.8 %copy-start = (bf16[1,512,2048]{2,1,0:T(8,128)(2,1)S(1)}, bf16[1,512,2048]{2,1,0:T(8,128)(2,1)}, u32[]{:S(2)}) copy-start(bf16[1,512,2048]{2,1,0:T(8,128)(2,1)} %param.7) | copy-start | bytes 6291460
  0.0 29.4 %collective-permute-start = (bf16[1,128,16,256]{3,2,1,0:T(8,128)(2,1)}, bf16[1,128,16,256]{3,2,1,0:T(8,128)(2,1)}, u32[]{:S(2)}, u32[]{:S(2)}) collective-permute-start(bf16[1,128,16,256]{3,2,1,0:T(8,128)(2,1)} %param.5), channel_id=1, source_target_pairs={{0,2},{2,4},{4,6},{6,0},{1,3},{3,5},{5,7},{7,1},{8,10},{10,12},{12... | collective-permute-start | bytes 3145736 | tf_op jit(solution)/shard_map/ppermute | solution.py:16
  3.0 47.4 %collective-permute-start.1 = (bf16[1,128,16,256]{3,2,1,0:T(8,128)(2,1)}, bf16[1,128,16,256]{3,2,1,0:T(8,128)(2,1)}, u32[]{:S(2)}, u32[]{:S(2)}) collective-permute-start(bf16[1,128,16,256]{3,2,1,0:T(8,128)(2,1)} %param.5), channel_id=1, source_target_pairs={{2,0},{4,2},{6,4},{0,6},{3,1},{5,3},{7,5},{1,7},{10,8},{12,10},{14... | collective-permute-start | bytes 3145736 | tf_op jit(solution)/shard_map/ppermute | solution.py:17
  5.8 3.4 %copy-start.1 = (bf16[1,128,16,256]{3,2,1,0:T(8,128)(2,1)S(1)}, bf16[1,128,16,256]{3,2,1,0:T(8,128)(2,1)}, u32[]{:S(2)}) copy-start(bf16[1,128,16,256]{3,2,1,0:T(8,128)(2,1)} %param.5) | copy-start | bytes 3145732
  5.8 3.4 %copy-start.3 = (bf16[1,64,8]{1,2,0:T(8,128)(2,1)S(1)}, bf16[1,64,8]{1,2,0:T(8,128)(2,1)}, u32[]{:S(2)}) copy-start(bf16[1,64,8]{1,2,0:T(8,128)(2,1)} %param.6) | copy-start | bytes 3076
  96.2 13.8 %copy-start.4 = (f32[1,16,256]{2,1,0:T(8,128)S(1)}, f32[1,16,256]{2,1,0:T(8,128)}, u32[]{:S(2)}) copy-start(f32[1,16,256]{2,1,0:T(8,128)} %param.8) | copy-start | bytes 49156
  108.4 1.0 copy-start.2
  111.6 14.3 %collective-permute-start.2 = (bf16[128,16,256]{2,1,0:T(8,128)(2,1)S(1)}, bf16[128,16,256]{2,1,0:T(8,128)(2,1)S(1)}, u32[]{:S(2)}, u32[]{:S(2)}) collective-permute-start(bf16[128,16,256]{2,1,0:T(8,128)(2,1)S(1)} %multiply_convert_fusion), channel_id=1, source_target_pairs={{0,8},{8,16},{16,24},{24,0},{1,9},{9,17},{17,25},{25,1},{2,10},{10... | collective-permute-start | bytes 3145736 | tf_op jit(solution)/shard_map/ppermute | solution.py:24
where the time goes:
time: 127 us
  waiting for transfers between devices  53.5 us (42%)
  blocking collectives  43.6 us (34%)
  matrix products  11.8 us (9%)
  local copies, waits for them, and re-layouts  8.1 us (6%)
  starting transfers between devices  5.16 us (4%)
  other arithmetic  4.59 us (4%)
    all_gather x1, blocking collectives, shards(): lax.all_gather(rank_rows[None], ('field', 'row'), axis=0, tiled=True)  31.4 us
    ppermute x1, waiting for transfers between devices, padded(): before = lax.ppermute(last, axis, up)  19.8 us
    ppermute x1, waiting for transfers between devices, padded(): after = lax.ppermute(initial, axis, down)  19.5 us
    ppermute x1, waiting for transfers between devices, from_behind(): lax.ppermute(array, axis, [(i, (i + by) % count) for i in range(count)])  14.2 us
    all_to_all x1, blocking collectives, shards(): lax.all_to_all(local_mix, 'row', split_axis=0, concat_axis=1, tiled=True)  12.2 us
    dot_general x1, matrix products, shards(): jnp.einsum('mrc,mcd->mrd', pieces, chosen, preferred_element_type=jnp.flo...  3.5 us
    dot_general x3, matrix products, squeeze_block(): jnp.einsum('ak,rae->rke', block_weights, block_panel, preferred_element_t...  3.5 us
    dot_general x1, matrix products, shards(): placed = jnp.einsum('mg,mrd->grd', selector, contrib)  3.09 us
  transfers between devices with their start and end apart: 3, of which 3 were waited for; matrix products, arithmetic and copies ran while one was open for 5% of the time, Pallas kernels for 0%

commit v1 on v0

v1 whole, which is shorter than its diff:
```python
import functools
import math

import jax
import jax.numpy as jnp
from jax import lax
from jax.experimental import pallas as pl
from jax.experimental.pallas import tpu as pltpu
from jax.sharding import PartitionSpec as P

MESH = pl.DeviceIdType.MESH
BF16, F32 = jnp.bfloat16, jnp.float32


def dot(a, b, dims=((1,), (0,))):
    return lax.dot_general(a, b, (dims, ((), ())), preferred_element_type=F32)


def grid_of(shape):
    return (
        lax.broadcasted_iota(jnp.int32, shape, 0),
        lax.broadcasted_iota(jnp.int32, shape, 1),
    )


def kernel(
    sizes,
    emb_hbm, compress_ref, mix_hbm, gain_ref, flags_ref,
    out_ref,
    emb, mix, own, near, inter, gathered, mixed, back, spread, done,
    emb_sem, mix_sem,
    near_send, near_recv,
    gat_send, gat_recv,
    back_send, back_recv,
    out_send, out_recv,
):
    segments, owners, groups, rows, fields, width, rank, chunks, group = sizes
    seg = lax.axis_index("segment")
    fld = lax.axis_index("field")
    row = lax.axis_index("row")
    part = rows // chunks
    span = fields * rank
    each = fields // groups
    blocks = part // group
    before, after = lax.rem(fld + owners - 1, owners), lax.rem(fld + 1, owners)

    loads = []
    for c in range(chunks):
        rng = pl.ds(c * part * fields, part * fields)
        load = pltpu.make_async_copy(emb_hbm.at[rng], emb.at[rng], emb_sem.at[c])
        load.start()
        loads.append(load)
    mix_load = pltpu.make_async_copy(mix_hbm, mix, mix_sem)
    mix_load.start()

    barrier = pltpu.get_barrier_semaphore()
    peers = []
    for i in range(owners):
        for j in range(groups):
            if i or j:
                peers.append((seg, lax.rem(fld + i, owners), lax.rem(row + j, groups)))
    for peer in peers:
        pl.semaphore_signal(barrier, inc=1, device_id=peer, device_id_type=MESH)
    ahead = (lax.rem(seg + 1, segments), fld, row)
    behind = (lax.rem(seg + segments - 1, segments), fld, row)
    for peer in (ahead, behind):
        pl.semaphore_signal(barrier, inc=1, device_id=peer, device_id_type=MESH)

    start = pl.multiple_of(fld * fields, fields)
    block_weights = compress_ref[pl.ds(start, fields), :]
    a, b = grid_of((group * rank, rank))
    tall = dot((a % rank == b).astype(BF16), block_weights, ((1,), (1,))).astype(BF16)
    a, b = grid_of((fields, group * fields))
    wide = dot(tall, (b % fields == a).astype(BF16))
    a, b = grid_of((group * rank, group * fields))
    squeeze = jnp.where(a // rank == b // fields, wide, 0.0).astype(BF16)

    def reduce_chunk(c):
        loads[c].wait()
        for g in range(blocks):
            src = (c * blocks + g) * group * fields
            dst = (c * blocks + g) * group * rank
            own[dst : dst + group * rank, :] = dot(
                squeeze, emb[src : src + group * fields, :]
            ).astype(BF16)

    sends = []

    def send_chunk(c):
        rng = pl.ds(c * part * rank, part * rank)
        for side, target in ((0, after), (1, before)):
            copy = pltpu.make_async_remote_copy(
                src_ref=own.at[rng],
                dst_ref=near.at[side, rng],
                send_sem=near_send.at[side, c],
                recv_sem=near_recv.at[side, c],
                device_id=(seg, target, row),
                device_id_type=MESH,
            )
            copy.start()
            sends.append(copy)

    reduce_chunk(0)
    pl.semaphore_wait(barrier, len(peers) + 2)
    send_chunk(0)
    for c in range(1, chunks):
        reduce_chunk(c)
        send_chunk(c)

    weight = [flags_ref[0, o].astype(F32) for o in range(3)]
    a, b = grid_of((group * fields, group * rank))
    same_row = a // fields == b // rank
    a, b = grid_of((group * rank, span))
    repeat = (a % rank == b % rank).astype(BF16)
    a, b = grid_of((group * fields, span))
    same_field = a % fields == b // rank
    a, b = grid_of((group, group * fields))
    fold = (b // fields == a).astype(BF16)
    scale = 1.0 / math.sqrt(width)

    gats = []

    def interact(c):
        for side in range(2):
            sends[2 * c + side].wait_recv()
        for g in range(blocks):
            src = (c * blocks + g) * group * fields
            dst = (c * blocks + g) * group * rank
            rng = slice(dst, dst + group * rank)
            partner = (
                weight[0] * near[0, rng, :].astype(F32)
                + weight[1] * own[rng, :].astype(F32)
                + weight[2] * near[1, rng, :].astype(F32)
            ).astype(BF16)
            prod = dot(emb[src : src + group * fields, :], partner, ((1,), (1,)))
            prod = jnp.where(same_row, prod * scale, 0.0).astype(BF16)
            prod = jnp.where(same_field, dot(prod, repeat), 0.0).astype(BF16)
            inter[c, g * group : (g + 1) * group, :] = dot(fold, prod).astype(BF16)
        place = gathered.at[
            c,
            pl.ds(pl.multiple_of(row * part, part), part),
            pl.ds(pl.multiple_of(fld * span, span), span),
        ]
        for i, peer in enumerate(peers):
            copy = pltpu.make_async_remote_copy(
                src_ref=inter.at[c],
                dst_ref=place,
                send_sem=gat_send.at[c, i],
                recv_sem=gat_recv.at[c],
                device_id=peer,
                device_id_type=MESH,
            )
            copy.start()
            gats.append(copy)
        pltpu.make_async_copy(inter.at[c], place, gat_recv.at[c]).start()

    backs = {}

    def project(c):
        pltpu.make_async_copy(gathered.at[c], gathered.at[c], gat_recv.at[c]).wait()
        if c == 0:
            mix_load.wait()
        cols = each * width
        step = min(cols, 512)
        for n in range(0, cols, step):
            mixed[c, :, n : n + step] = dot(
                gathered[c], mix[:, n : n + step]
            ).astype(BF16)
        for j in range(1, groups):
            to = lax.rem(row + j, groups)
            copy = pltpu.make_async_remote_copy(
                src_ref=mixed.at[c, pl.ds(pl.multiple_of(to * part, part), part)],
                dst_ref=back.at[c, j - 1],
                send_sem=back_send.at[c, j - 1],
                recv_sem=back_recv.at[c, j - 1],
                device_id=(seg, fld, to),
                device_id_type=MESH,
            )
            copy.start()
            backs[c, j] = copy

    outs = []

    def finish(c):
        for j in range(groups):
            source = lax.rem(row + groups - j, groups)
            if j:
                backs[c, j].wait_recv()
            for f in range(each):
                lanes = slice(f * width, (f + 1) * width)
                if j:
                    piece = back[c, j - 1, :, lanes]
                else:
                    mine = pl.ds(pl.multiple_of(row * part, part), part)
                    piece = mixed[c, mine, lanes]
                piece = piece.astype(F32)
                for l in range(width // 128):
                    spread[l, pl.ds(source * each + f, part, stride=fields), :] = piece[
                        :, l * 128 : (l + 1) * 128
                    ]
        gain = gain_ref[...][None]
        size = 8 * fields
        for i in range(part // 8):
            at = c * part * fields + i * size
            here = slice(i * size, (i + 1) * size)
            summed = emb[at : at + size, :].astype(F32) + jnp.concatenate(
                [spread[l, here, :] for l in range(width // 128)], axis=1
            )
            mean = jnp.sum(summed * summed, axis=-1, keepdims=True) * (1.0 / width)
            normed = summed * lax.rsqrt(mean + 1e-06)
            normed = normed.reshape(8, fields, width) * gain
            done[at : at + size, :] = normed.reshape(size, width).astype(BF16)
        rng = pl.ds(c * part * fields, part * fields)
        copy = pltpu.make_async_remote_copy(
            src_ref=done.at[rng],
            dst_ref=out_ref.at[rng],
            send_sem=out_send.at[c],
            recv_sem=out_recv.at[c],
            device_id=ahead,
            device_id_type=MESH,
        )
        copy.start()
        outs.append(copy)

    for c in range(chunks + 2):
        if c < chunks:
            interact(c)
        if 0 <= c - 2:
            finish(c - 2)
        if 0 <= c - 1 < chunks:
            project(c - 1)

    for copy in sends:
        copy.wait_send()
    for copy in gats:
        copy.wait_send()
    for copy in backs.values():
        copy.wait_send()
    for copy in outs:
        copy.wait()


def shards(embeddings, compress, mixing, gain, flags):
    _, rows, fields, width = embeddings.shape
    segments, owners, groups = (lax.axis_size(n) for n in ("segment", "field", "row"))
    rank = compress.shape[2]
    chunks, group = 4, 16
    part = rows // chunks
    depth, cols = mixing.shape[1:]
    sizes = (segments, owners, groups, rows, fields, width, rank, chunks, group)
    vmem = pl.BlockSpec(memory_space=pltpu.VMEM)
    hbm = pl.BlockSpec(memory_space=pl.ANY)
    dma = pltpu.SemaphoreType.DMA
    others = max(groups - 1, 1)
    out = pl.pallas_call(
        functools.partial(kernel, sizes),
        out_shape=jax.ShapeDtypeStruct((rows * fields, width), BF16),
        in_specs=[hbm, vmem, hbm, vmem, pl.BlockSpec(memory_space=pltpu.SMEM)],
        out_specs=hbm,
        scratch_shapes=[
            pltpu.VMEM((rows * fields, width), BF16),
            pltpu.VMEM((depth, cols), BF16),
            pltpu.VMEM((rows * rank, width), BF16),
            pltpu.VMEM((2, rows * rank, width), BF16),
            pltpu.VMEM((chunks, part, fields * rank), BF16),
            pltpu.VMEM((chunks, groups * part, depth), BF16),
            pltpu.VMEM((chunks, groups * part, cols), BF16),
            pltpu.VMEM((chunks, others, part, cols), BF16),
            pltpu.VMEM((width // 128, part * fields, 128), F32),
            pltpu.VMEM((rows * fields, width), BF16),
            dma((chunks,)),
            dma,
            dma((2, chunks)),
            dma((2, chunks)),
            dma((chunks, owners * groups - 1)),
            dma((chunks,)),
            dma((chunks, others)),
            dma((chunks, others)),
            dma((chunks,)),
            dma((chunks,)),
        ],
        compiler_params=pltpu.CompilerParams(
            collective_id=0, has_side_effects=True, vmem_limit_bytes=48 * 2**20
        ),
    )(
        embeddings.reshape(rows * fields, width),
        compress[0],
        mixing[0],
        gain[0],
        flags,
    )
    return out.reshape(1, rows, fields, width)


def solution(mesh):
    placed = (
        P("segment", "row", "field", None),
        P("segment", None, None),
        P("segment", None, ("field", "row")),
        P("segment", "field", None),
        P("field", None),
    )
    return jax.shard_map(
        shards,
        mesh=mesh,
        in_specs=placed,
        out_specs=P("segment", "row", "field", None),
        check_vma=False,
    )
```

time: 127 us -> 61.9 us (0.49)
  Pallas kernels: 0 us -> 55.7 us
  waiting for transfers between devices: 53.5 us -> 0 us
  blocking collectives: 43.6 us -> 0 us
  matrix products: 11.8 us -> 0 us
  starting transfers between devices: 5.16 us -> 0 us
  other arithmetic: 4.59 us -> 0 us
  local copies, waits for them, and re-layouts: 8.1 us -> 5.94 us
    pallas_call x0 -> x1, Pallas kernels: none -> 55.7 us  [shards(): pl.pallas_call(functools.partial(kernel, sizes), out_shape=jax.ShapeDtype...]
    ppermute x3 -> x0, waiting for transfers between devices: 53.5 us -> none  [the longest x1 19.8 us: padded(): before = lax.ppermute(last, axis, up)]
    all_gather x1 -> x0, blocking collectives: 31.4 us -> none  [shards(): lax.all_gather(rank_rows[None], ('field', 'row'), axis=0, tiled=True)]
    all_to_all x1 -> x0, blocking collectives: 12.2 us -> none  [shards(): lax.all_to_all(local_mix, 'row', split_axis=0, concat_axis=1, tiled=True)]
    dot_general x6 -> x0, matrix products: 11.8 us -> none  [the longest x1 3.5 us: shards(): jnp.einsum('mrc,mcd->mrd', pieces, chosen, preferred_element_type=jnp.flo...]
    ppermute x3 -> x0, starting transfers between devices: 5.16 us -> none  [the longest x1 3.02 us: padded(): before = lax.ppermute(last, axis, up)]
    unnamed x12 -> x10, local copies, waits for them, and re-layouts: 2.26 us -> 5.94 us
    gather x1 -> x0, local copies, waits for them, and re-layouts: 2.76 us -> none  [shards(): chosen = jnp.take(slabs, owner_ids, axis=0)]
  transfers between devices with their start and end apart: 3 -> 0, of which waited for: 3 -> 0; matrix products, arithmetic and copies ran while one was open for 5% -> 0% of each run, Pallas kernels for 0% -> 0%
where the time goes in v1:
time: 61.9 us; the launch traced here: 61.6 us
  Pallas kernels  55.7 us (90%)
  local copies, waits for them, and re-layouts  5.94 us (10%)
    pallas_call x1, Pallas kernels, shards(): pl.pallas_call(functools.partial(kernel, sizes), out_shape=jax.ShapeDtype...  55.7 us
    unnamed x10, local copies, waits for them, and re-layouts  5.94 us

profile of v1, /device:TPU:0, one launch (start us, length us, event | category | flops | bytes accessed | tf_op | source)
XLA Modules:
  0.0 61.6 jit_solution(14297160125837857460)
XLA Ops:
  0.0 0.8 %copy.6 = bf16[1,64,8]{2,1,0:T(8,128)(2,1)S(1)} copy(bf16[1,64,8]{1,2,0:T(8,128)(2,1)} %param.6) | data formatting | bytes 2048 | tf_op args[1]
  0.8 0.0 copy-start
  0.8 1.6 %copy-done = bf16[1,512,2048]{2,1,0:T(8,128)(2,1)S(1)} copy-done((bf16[1,512,2048]{2,1,0:T(8,128)(2,1)S(1)}, bf16[1,512,2048]{2,1,0:T(8,128)(2,1)}, u32[]{:S(2)}) %copy-start) | copy-done | bytes 2097176
  2.4 0.0 copy-start.1
  2.4 1.2 %copy-done.1 = bf16[1,128,16,256]{3,2,1,0:T(8,128)(2,1)S(1)} copy-done((bf16[1,128,16,256]{3,2,1,0:T(8,128)(2,1)S(1)}, bf16[1,128,16,256]{3,2,1,0:T(8,128)(2,1)}, u32[]{:S(2)}) %copy-start.1) | copy-done | bytes 1048600
  3.6 0.0 copy-start.2
  3.6 0.7 %copy-done.2 = f32[1,16,256]{2,1,0:T(8,128)S(1)} copy-done((f32[1,16,256]{2,1,0:T(8,128)S(1)}, f32[1,16,256]{2,1,0:T(8,128)}, u32[]{:S(2)}) %copy-start.2) | copy-done | bytes 16408
  4.3 0.0 copy-start.3
  4.3 0.7 %copy-done.3 = s32[1,3]{1,0:T(1,128)S(1)} copy-done((s32[1,3]{1,0:T(1,128)S(1)}, s32[1,3]{1,0:T(1,128)}, u32[]{:S(2)}) %copy-start.3) | copy-done | bytes 36
  5.0 55.7 %shard_map.55 = bf16[2048,256]{1,0:T(8,128)(2,1)S(1)} custom-call(bf16[2048,256]{1,0:T(8,128)(2,1)S(1)} %bitcast.7, bf16[64,8]{1,0:T(8,128)(2,1)S(1)} %bitcast.8, bf16[512,2048]{1,0:T(8,128)(2,1)S(1)} %bitcast.6, f32[16,256]{1,0:T(8,128)S(1)} %bitcast.9, s32[1,3]{1,0:T(1,128)S(1)} %copy-done.3), custom_call_target="tpu_custom_call" | custom-call | tf_op jit(solution)/shard_map/pallas_call | solution.py:255
  60.6 1.0 %copy.8 = bf16[1,128,16,256]{3,2,1,0:T(8,128)(2,1)} copy(bf16[1,128,16,256]{3,2,1,0:T(8,128)(2,1)S(1)} %bitcast.5) | data formatting | bytes 2097152
Async XLA Ops:
  0.8 1.6 %copy-start = (bf16[1,512,2048]{2,1,0:T(8,128)(2,1)S(1)}, bf16[1,512,2048]{2,1,0:T(8,128)(2,1)}, u32[]{:S(2)}) copy-start(bf16[1,512,2048]{2,1,0:T(8,128)(2,1)} %param.7) | copy-start | bytes 6291460
  2.4 1.2 %copy-start.1 = (bf16[1,128,16,256]{3,2,1,0:T(8,128)(2,1)S(1)}, bf16[1,128,16,256]{3,2,1,0:T(8,128)(2,1)}, u32[]{:S(2)}) copy-start(bf16[1,128,16,256]{3,2,1,0:T(8,128)(2,1)} %param.5) | copy-start | bytes 3145732
  3.6 0.7 %copy-start.2 = (f32[1,16,256]{2,1,0:T(8,128)S(1)}, f32[1,16,256]{2,1,0:T(8,128)}, u32[]{:S(2)}) copy-start(f32[1,16,256]{2,1,0:T(8,128)} %param.8) | copy-start | bytes 49156
  4.3 0.7 %copy-start.3 = (s32[1,3]{1,0:T(1,128)S(1)}, s32[1,3]{1,0:T(1,128)}, u32[]{:S(2)}) copy-start(s32[1,3]{1,0:T(1,128)} %flags_ref.1) | copy-start | bytes 40

commit v2 on v1

--- a/solution.py
+++ b/solution.py
@@ -8,6 +8,7 @@
 from jax.experimental.pallas import tpu as pltpu
 from jax.sharding import PartitionSpec as P
 
+AHEAD = 1
 MESH = pl.DeviceIdType.MESH
 BF16, F32 = jnp.bfloat16, jnp.float32
 
@@ -25,10 +26,10 @@
 
 def kernel(
     sizes,
-    emb_hbm, compress_ref, mix_hbm, gain_ref, flags_ref,
+    emb_hbm, compress_hbm, mix_hbm, gain_hbm, flags_hbm,
     out_ref,
-    emb, mix, own, near, inter, gathered, mixed, back, spread, done,
-    emb_sem, mix_sem,
+    emb, compress_ref, mix, gain_ref, flags_ref, own, near, inter, gathered, mixed, back, spread, done,
+    emb_sem, mix_sem, small_sem,
     near_send, near_recv,
     gat_send, gat_recv,
     back_send, back_recv,
@@ -44,6 +45,18 @@
     blocks = part // group
     before, after = lax.rem(fld + owners - 1, owners), lax.rem(fld + 1, owners)
 
+    smalls = [
+        pltpu.make_async_copy(src, dst, small_sem.at[i])
+        for i, (src, dst) in enumerate(
+            (
+                (compress_hbm, compress_ref),
+                (gain_hbm, gain_ref),
+                (flags_hbm, flags_ref),
+            )
+        )
+    ]
+    for load in smalls:
+        load.start()
     loads = []
     for c in range(chunks):
         rng = pl.ds(c * part * fields, part * fields)
@@ -66,12 +79,12 @@
     for peer in (ahead, behind):
         pl.semaphore_signal(barrier, inc=1, device_id=peer, device_id_type=MESH)
 
-    start = pl.multiple_of(fld * fields, fields)
-    block_weights = compress_ref[pl.ds(start, fields), :]
+    a, b = grid_of((compress_ref.shape[1], group * fields))
+    pick = (a == fld * fields + b % fields).astype(BF16)
     a, b = grid_of((group * rank, rank))
-    tall = dot((a % rank == b).astype(BF16), block_weights, ((1,), (1,))).astype(BF16)
-    a, b = grid_of((fields, group * fields))
-    wide = dot(tall, (b % fields == a).astype(BF16))
+    repeat = (a % rank == b).astype(BF16)
+    smalls[0].wait()
+    wide = dot(repeat, dot(compress_ref[...], pick).astype(BF16))
     a, b = grid_of((group * rank, group * fields))
     squeeze = jnp.where(a // rank == b // fields, wide, 0.0).astype(BF16)
 
@@ -105,8 +118,10 @@
     send_chunk(0)
     for c in range(1, chunks):
         reduce_chunk(c)
-        send_chunk(c)
-
+        if c < AHEAD:
+            send_chunk(c)
+
+    smalls[2].wait()
     weight = [flags_ref[0, o].astype(F32) for o in range(3)]
     a, b = grid_of((group * fields, group * rank))
     same_row = a // fields == b // rank
@@ -123,6 +138,10 @@
     def interact(c):
         for side in range(2):
             sends[2 * c + side].wait_recv()
+        if c + AHEAD < chunks:
+            for side in range(2):
+                sends[2 * c + side].wait_send()
+            send_chunk(c + AHEAD)
         for g in range(blocks):
             src = (c * blocks + g) * group * fields
             dst = (c * blocks + g) * group * rank
@@ -160,6 +179,7 @@
         pltpu.make_async_copy(gathered.at[c], gathered.at[c], gat_recv.at[c]).wait()
         if c == 0:
             mix_load.wait()
+            smalls[1].wait()
         cols = each * width
         step = min(cols, 512)
         for n in range(0, cols, step):
@@ -230,7 +250,7 @@
         if 0 <= c - 1 < chunks:
             project(c - 1)
 
-    for copy in sends:
+    for copy in sends[-2 * AHEAD :]:
         copy.wait_send()
     for copy in gats:
         copy.wait_send()
@@ -248,18 +268,20 @@
     part = rows // chunks
     depth, cols = mixing.shape[1:]
     sizes = (segments, owners, groups, rows, fields, width, rank, chunks, group)
-    vmem = pl.BlockSpec(memory_space=pltpu.VMEM)
     hbm = pl.BlockSpec(memory_space=pl.ANY)
     dma = pltpu.SemaphoreType.DMA
     others = max(groups - 1, 1)
     out = pl.pallas_call(
         functools.partial(kernel, sizes),
         out_shape=jax.ShapeDtypeStruct((rows * fields, width), BF16),
-        in_specs=[hbm, vmem, hbm, vmem, pl.BlockSpec(memory_space=pltpu.SMEM)],
+        in_specs=[hbm] * 5,
         out_specs=hbm,
         scratch_shapes=[
             pltpu.VMEM((rows * fields, width), BF16),
+            pltpu.VMEM((rank, compress.shape[1]), BF16),
             pltpu.VMEM((depth, cols), BF16),
+            pltpu.VMEM((fields, width), F32),
+            pltpu.SMEM(flags.shape, jnp.int32),
             pltpu.VMEM((rows * rank, width), BF16),
             pltpu.VMEM((2, rows * rank, width), BF16),
             pltpu.VMEM((chunks, part, fields * rank), BF16),
@@ -270,6 +292,7 @@
             pltpu.VMEM((rows * fields, width), BF16),
             dma((chunks,)),
             dma,
+            dma((3,)),
             dma((2, chunks)),
             dma((2, chunks)),
             dma((chunks, owners * groups - 1)),
@@ -280,11 +303,11 @@
             dma((chunks,)),
         ],
         compiler_params=pltpu.CompilerParams(
-            collective_id=0, has_side_effects=True, vmem_limit_bytes=48 * 2**20
+            collective_id=0, has_side_effects=True, vmem_limit_bytes=60 * 2**20
         ),
     )(
         embeddings.reshape(rows * fields, width),
-        compress[0],
+        compress[0].T,
         mixing[0],
         gain[0],
         flags,

time: 61.9 us -> 51.6 us (0.83)
  Pallas kernels: 55.7 us -> 49.2 us
  local copies, waits for them, and re-layouts: 5.94 us -> 2.26 us
    pallas_call x1, Pallas kernels: 55.7 us -> 49.2 us  [shards(): pl.pallas_call(functools.partial(kernel, sizes), out_shape=jax.ShapeDtype...]
    unnamed x10 -> x1, local copies, waits for them, and re-layouts: 5.94 us -> 2.26 us
where the time goes in v2:
time: 51.6 us; the launch traced here: 51.4 us
  Pallas kernels  49.2 us (95%)
  local copies, waits for them, and re-layouts  2.26 us (4%)
    pallas_call x1, Pallas kernels, shards(): pl.pallas_call(functools.partial(kernel, sizes), out_shape=jax.ShapeDtype...  49.2 us
    unnamed x1, local copies, waits for them, and re-layouts  2.26 us

profile of v2, /device:TPU:0, one launch (start us, length us, event | category | flops | bytes accessed | tf_op | source)
XLA Modules:
  0.0 51.4 jit_solution(9066091199096504307)
XLA Ops:
  0.0 49.2 %shard_map.55 = bf16[2048,256]{1,0:T(8,128)(2,1)} custom-call(bf16[2048,256]{1,0:T(8,128)(2,1)} %bitcast.9, bf16[8,64]{1,0:T(8,128)(2,1)} %bitcast.11, bf16[512,2048]{1,0:T(8,128)(2,1)} %bitcast.8, f32[16,256]{1,0:T(8,128)} %bitcast.10, s32[1,3]{1,0:T(1,128)} %flags_hbm.1), custom_call_target="tpu_custom_call" | custom-call | tf_op jit(solution)/shard_map/pallas_call | solution.py:274
  49.2 2.3 %copy.7 = bf16[1,128,16,256]{3,2,1,0:T(8,128)(2,1)} copy(bf16[1,128,16,256]{3,2,1,0:T(8,128)(2,1)} %bitcast.7) | data formatting | bytes 2097152

commit v3 on v2

v3 whole, which is shorter than its diff:
```python
import functools
import math

import jax
import jax.numpy as jnp
from jax import lax
from jax.experimental import pallas as pl
from jax.experimental.pallas import tpu as pltpu
from jax.sharding import PartitionSpec as P

AHEAD = 2
CHUNK = 32
MESH = pl.DeviceIdType.MESH
BF16, F32 = jnp.bfloat16, jnp.float32


def dot(a, b, dims=((1,), (0,))):
    return lax.dot_general(a, b, (dims, ((), ())), preferred_element_type=F32)


def grid_of(shape):
    return (
        lax.broadcasted_iota(jnp.int32, shape, 0),
        lax.broadcasted_iota(jnp.int32, shape, 1),
    )


def kernel(
    sizes, parts,
    emb_hbm, compress_hbm, mix_hbm, gain_hbm, flags_hbm,
    out_ref,
    emb, compress_ref, mix, gain_ref, flags_ref,
    own, near, inter, gathered, mixed, back, spread, done,
    emb_sem, mix_sem, small_sem,
    near_send, near_recv,
    gat_send, gat_recv,
    back_send, back_recv,
    out_send, out_recv,
):
    segments, owners, groups, rows, fields, width, rank, group = sizes
    seg = lax.axis_index("segment")
    fld = lax.axis_index("field")
    row = lax.axis_index("row")
    span = fields * rank
    each = fields // groups
    tall_in, tall_out = group * fields, group * rank
    pieces = rows // group
    before, after = lax.rem(fld + owners - 1, owners), lax.rem(fld + 1, owners)

    smalls = [
        pltpu.make_async_copy(src, dst, small_sem.at[i])
        for i, (src, dst) in enumerate(
            (
                (compress_hbm, compress_ref),
                (gain_hbm, gain_ref),
                (flags_hbm, flags_ref),
            )
        )
    ]
    for load in smalls:
        load.start()
    loads = []
    for p in range(pieces):
        rng = pl.ds(p * tall_in, tall_in)
        load = pltpu.make_async_copy(emb_hbm.at[rng], emb.at[rng], emb_sem.at[p])
        load.start()
        loads.append(load)
    mix_load = pltpu.make_async_copy(mix_hbm, mix, mix_sem)
    mix_load.start()

    barrier = pltpu.get_barrier_semaphore()
    ahead = (lax.rem(seg + 1, segments), fld, row)
    behind = (lax.rem(seg + segments - 1, segments), fld, row)
    peers = [
        (seg, lax.rem(fld + i, owners), lax.rem(row + j, groups))
        for i in range(owners)
        for j in range(groups)
        if i or j
    ]
    greeted = peers + [ahead, behind]
    for peer in greeted:
        pl.semaphore_signal(barrier, inc=1, device_id=peer, device_id_type=MESH)

    a, b = grid_of((compress_ref.shape[1], tall_in))
    pick = (a == fld * fields + b % fields).astype(BF16)
    a, b = grid_of((tall_out, rank))
    repeat = (a % rank == b).astype(BF16)
    smalls[0].wait()
    wide = dot(repeat, dot(compress_ref[...], pick).astype(BF16))
    a, b = grid_of((tall_out, tall_in))
    squeeze = jnp.where(a // rank == b // fields, wide, 0.0).astype(BF16)

    def reduce_piece(p):
        loads[p].wait()
        own[p * tall_out : (p + 1) * tall_out, :] = dot(
            squeeze, emb[p * tall_in : (p + 1) * tall_in, :]
        ).astype(BF16)

    sends = []

    def send_piece(p):
        rng = pl.ds(p * tall_out, tall_out)
        for side, target in ((0, after), (1, before)):
            copy = pltpu.make_async_remote_copy(
                src_ref=own.at[rng],
                dst_ref=near.at[side, rng],
                send_sem=near_send.at[side, p],
                recv_sem=near_recv.at[side, p],
                device_id=(seg, target, row),
                device_id_type=MESH,
            )
            copy.start()
            sends.append(copy)

    reduce_piece(0)
    pl.semaphore_wait(barrier, len(greeted))
    send_piece(0)
    for p in range(1, pieces):
        reduce_piece(p)
        if p < AHEAD:
            send_piece(p)

    smalls[2].wait()
    weight = [flags_ref[0, o].astype(F32) for o in range(3)]
    a, b = grid_of((tall_in, tall_out))
    same_row = a // fields == b // rank
    a, b = grid_of((tall_out, span))
    repeat = (a % rank == b % rank).astype(BF16)
    a, b = grid_of((tall_in, span))
    same_field = a % fields == b // rank
    a, b = grid_of((group, tall_in))
    fold = (b // fields == a).astype(BF16)
    scale = 1.0 / math.sqrt(width)

    def place_of(c, source):
        first, part = parts[c]
        at = groups * first + source * part
        return pl.ds(pl.multiple_of(at, group), part)

    columns = pl.ds(pl.multiple_of(fld * span, span), span)

    def interact(c, p):
        for side in range(2):
            sends[2 * p + side].wait_recv()
        if p + AHEAD < pieces:
            for side in range(2):
                sends[2 * p + side].wait_send()
            send_piece(p + AHEAD)
        rng = slice(p * tall_out, (p + 1) * tall_out)
        partner = (
            weight[0] * near[0, rng, :].astype(F32)
            + weight[1] * own[rng, :].astype(F32)
            + weight[2] * near[1, rng, :].astype(F32)
        ).astype(BF16)
        prod = dot(emb[p * tall_in : (p + 1) * tall_in, :], partner, ((1,), (1,)))
        prod = jnp.where(same_row, prod * scale, 0.0).astype(BF16)
        prod = jnp.where(same_field, dot(prod, repeat), 0.0).astype(BF16)
        inter[p * group : (p + 1) * group, :] = dot(fold, prod).astype(BF16)

    gats = []

    def gather(c):
        piece = inter.at[pl.ds(*parts[c])]
        slot = gathered.at[place_of(c, row), columns]
        pltpu.make_async_copy(piece, slot, gat_recv.at[c]).start()
        for i, peer in enumerate(peers):
            copy = pltpu.make_async_remote_copy(
                src_ref=piece,
                dst_ref=slot,
                send_sem=gat_send.at[c, i],
                recv_sem=gat_recv.at[c],
                device_id=peer,
                device_id_type=MESH,
            )
            copy.start()
            gats.append(copy)

    backs = {}

    def project(c):
        if c == 0:
            mix_load.wait()
            smalls[1].wait()
        first, part = parts[c]
        cols = each * width
        step = min(cols, 512)
        here = slice(groups * first, groups * (first + part))
        whole = gathered.at[pl.ds(groups * first, groups * part)]
        pltpu.make_async_copy(whole, whole, gat_recv.at[c]).wait()
        for n in range(0, cols, step):
            mixed[here, n : n + step] = dot(
                gathered[here, :], mix[:, n : n + step]
            ).astype(BF16)
        for j in range(1, groups):
            to = lax.rem(row + j, groups)
            copy = pltpu.make_async_remote_copy(
                src_ref=mixed.at[place_of(c, to)],
                dst_ref=back.at[j - 1, pl.ds(first, part)],
                send_sem=back_send.at[c, j - 1],
                recv_sem=back_recv.at[c, j - 1],
                device_id=(seg, fld, to),
                device_id_type=MESH,
            )
            copy.start()
            backs[c, j] = copy

    outs = []

    def finish(c):
        first, part = parts[c]
        for j in range(groups):
            source = lax.rem(row + groups - j, groups)
            if j:
                backs[c, j].wait_recv()
            for f in range(each):
                lanes = slice(f * width, (f + 1) * width)
                if j:
                    piece = back[j - 1, first : first + part, lanes]
                else:
                    piece = mixed[place_of(c, row), lanes]
                piece = piece.astype(F32)
                for l in range(width // 128):
                    spread[l, pl.ds(source * each + f, part, stride=fields), :] = piece[
                        :, l * 128 : (l + 1) * 128
                    ]
        gain = gain_ref[...][None]
        size = 8 * fields
        for i in range(part // 8):
            at = first * fields + i * size
            here = slice(i * size, (i + 1) * size)
            summed = emb[at : at + size, :].astype(F32) + jnp.concatenate(
                [spread[l, here, :] for l in range(width // 128)], axis=1
            )
            mean = jnp.sum(summed * summed, axis=-1, keepdims=True) * (1.0 / width)
            normed = summed * lax.rsqrt(mean + 1e-06)
            normed = normed.reshape(8, fields, width) * gain
            done[at : at + size, :] = normed.reshape(size, width).astype(BF16)
        rng = pl.ds(first * fields, part * fields)
        copy = pltpu.make_async_remote_copy(
            src_ref=done.at[rng],
            dst_ref=out_ref.at[rng],
            send_sem=out_send.at[c],
            recv_sem=out_recv.at[c],
            device_id=ahead,
            device_id_type=MESH,
        )
        copy.start()
        outs.append(copy)

    last = len(parts) - 1
    for c, (first, part) in enumerate(parts):
        early = part > group
        for p in range(first // group, (first + part) // group):
            interact(c, p)
        gather(c)
        if c >= 2:
            finish(c - 2)
        if c:
            project(c - 1)
    if last:
        finish(last - 1)
    project(last)
    finish(last)

    for copy in sends[-2 * AHEAD :] + gats:
        copy.wait_send()
    for copy in backs.values():
        copy.wait_send()
    for copy in outs:
        copy.wait()


def shards(embeddings, compress, mixing, gain, flags):
    _, rows, fields, width = embeddings.shape
    segments, owners, groups = (lax.axis_size(n) for n in ("segment", "field", "row"))
    rank = compress.shape[2]
    group = 16
    depth, cols = mixing.shape[1:]
    parts, first = [], 0
    while first < rows:
        part = min(CHUNK, rows - first)
        parts.append((first, part))
        first += part
    chunks, pieces = len(parts), rows // group
    sizes = (segments, owners, groups, rows, fields, width, rank, group)
    hbm = pl.BlockSpec(memory_space=pl.ANY)
    dma = pltpu.SemaphoreType.DMA
    others = max(groups - 1, 1)
    out = pl.pallas_call(
        functools.partial(kernel, sizes, parts),
        out_shape=jax.ShapeDtypeStruct((rows * fields, width), BF16),
        in_specs=[hbm] * 5,
        out_specs=pl.BlockSpec(memory_space=pl.ANY),
        scratch_shapes=[
            pltpu.VMEM((rows * fields, width), BF16),
            pltpu.VMEM((rank, compress.shape[1]), BF16),
            pltpu.VMEM((depth, cols), BF16),
            pltpu.VMEM((fields, width), F32),
            pltpu.SMEM(flags.shape, jnp.int32),
            pltpu.VMEM((rows * rank, width), BF16),
            pltpu.VMEM((2, rows * rank, width), BF16),
            pltpu.VMEM((rows, fields * rank), BF16),
            pltpu.VMEM((groups * rows, depth), BF16),
            pltpu.VMEM((groups * rows, cols), BF16),
            pltpu.VMEM((others, rows, cols), BF16),
            pltpu.VMEM((width // 128, CHUNK * fields, 128), F32),
            pltpu.VMEM((rows * fields, width), BF16),
            dma((pieces,)),
            dma,
            dma((3,)),
            dma((2, pieces)),
            dma((2, pieces)),
            dma((chunks, owners * groups - 1)),
            dma((chunks,)),
            dma((chunks, others)),
            dma((chunks, others)),
            dma((chunks,)),
            dma((chunks,)),
        ],
        compiler_params=pltpu.CompilerParams(
            collective_id=0, has_side_effects=True, vmem_limit_bytes=60 * 2**20
        ),
    )(
        embeddings.reshape(rows * fields, width),
        compress[0].T,
        mixing[0],
        gain[0],
        flags,
    )
    return out.reshape(1, rows, fields, width)


def solution(mesh):
    placed = (
        P("segment", "row", "field", None),
        P("segment", None, None),
        P("segment", None, ("field", "row")),
        P("segment", "field", None),
        P("field", None),
    )
    return jax.shard_map(
        shards,
        mesh=mesh,
        in_specs=placed,
        out_specs=P("segment", "row", "field", None),
        check_vma=False,
    )
```

time: 51.6 us -> 49.1 us (0.952)
  Pallas kernels: 49.2 us -> 46.6 us
    pallas_call x1, Pallas kernels: 49.2 us -> 46.6 us  [shards(): pl.pallas_call(functools.partial(kernel, sizes, parts), out_shape=jax.Sha...]
where the time goes in v3:
time: 49.1 us; the launch traced here: 48.9 us
  Pallas kernels  46.6 us (95%)
  local copies, waits for them, and re-layouts  2.26 us (5%)
    pallas_call x1, Pallas kernels, shards(): pl.pallas_call(functools.partial(kernel, sizes, parts), out_shape=jax.Sha...  46.6 us
    unnamed x1, local copies, waits for them, and re-layouts  2.26 us

profile of v3, /device:TPU:0, one launch (start us, length us, event | category | flops | bytes accessed | tf_op | source)
XLA Modules:
  0.0 48.9 jit_solution(15858528040305173734)
XLA Ops:
  0.0 46.6 %shard_map.55 = bf16[2048,256]{1,0:T(8,128)(2,1)} custom-call(bf16[2048,256]{1,0:T(8,128)(2,1)} %bitcast.9, bf16[8,64]{1,0:T(8,128)(2,1)} %bitcast.11, bf16[512,2048]{1,0:T(8,128)(2,1)} %bitcast.8, f32[16,256]{1,0:T(8,128)} %bitcast.10, s32[1,3]{1,0:T(1,128)} %flags_hbm.1), custom_call_target="tpu_custom_call" | custom-call | tf_op jit(solution)/shard_map/pallas_call | solution.py:289
  46.6 2.3 %copy.7 = bf16[1,128,16,256]{3,2,1,0:T(8,128)(2,1)} copy(bf16[1,128,16,256]{3,2,1,0:T(8,128)(2,1)} %bitcast.7) | data formatting | bytes 2097152
